TPU v7x, 32 devices: a whole 2x2x4 slice. The times are simulated.
32 devices in a mesh: groups: 1, shard: 16 (over z, y, core), layer: 2 (over x).
Axes of the slice: x: 2, y: 2, z: 4, core: 2. Of those that a mesh axis runs over, the one named last changes fastest.
Arguments:
- train_grads: bfloat16 [8192, 2, 4096], P(('groups', 'shard'), 'layer'), may hold values from -0.049804688 to 0.049804688
- queries: bfloat16 [256, 2, 4096], P('shard', 'layer'), may hold values from -6 to 6
- basis_in: float32 [2, 64, 64], P('layer'), may hold values from -0.75 to 0.75
- basis_out: float32 [2, 64, 64], P('layer'), may hold values from -0.75 to 0.75
- eigen: float32 [2, 64, 64], P('layer'), may hold values from 0.05 to 5
Outputs:
- scores: float32 [8192, 256], P(('groups', 'shard'), 'layer')
All inputs are finite; a program needn't handle non-finite values.
Results may differ from a plain program's by a relative error of at most 0.0029.
Values may be sent and summed in bfloat16 or wider, within the bound.
A program may use at most 64 MiB of HBM per device.

v0:
```python
import jax
import jax.numpy as jnp
from jax import lax
from jax.sharding import PartitionSpec as P


def precondition(queries, basis_in, basis_out, eigen):
    count = queries.shape[0]
    layers = queries.shape[1]
    side = basis_in.shape[-1]
    grads = queries.astype(jnp.float32).reshape(count, layers, side, side)
    highest = lax.Precision.HIGHEST
    rotated = jnp.einsum("lai,qlab,lbj->qlij", basis_out, grads, basis_in, precision=highest)
    scaled = rotated / (eigen + 0.1)
    result = jnp.einsum("lia,qlab,ljb->qlij", basis_out, scaled, basis_in, precision=highest)
    return result.reshape(count, layers * side * side).astype(jnp.bfloat16)


def score_block(left, right):
    return lax.dot_general(
        left, right, (((1,), (1,)), ((), ())), preferred_element_type=jnp.float32
    )


def body(train_grads, queries, basis_in, basis_out, eigen):
    examples = train_grads.shape[0]
    train_flat = train_grads.reshape(examples, train_grads.shape[1] * train_grads.shape[2])
    precond = precondition(queries, basis_in, basis_out, eigen)
    gathered = lax.all_gather(precond, "shard", axis=0, tiled=True)
    mine = lax.psum_scatter(
        score_block(gathered, train_flat), "layer", scatter_dimension=0, tiled=True
    )
    return jnp.transpose(mine)


def solution(mesh):
    placed = (
        P(("groups", "shard"), "layer", None),
        P("shard", "layer", None),
        P("layer", None, None),
        P("layer", None, None),
        P("layer", None, None),
    )
    return jax.shard_map(
        body, mesh=mesh, in_specs=placed, out_specs=P(("groups", "shard"), "layer"), check_vma=False
    )
```

profile of v0, /device:TPU:1, one launch (start us, length us, event | category | flops | bytes accessed | tf_op | source)
XLA Modules:
  0.0 84.3 jit_solution(3987353257771639253)
XLA Ops:
  6.5 0.0 copy-start
  6.5 0.0 all-gather.2.cloned.1.call-start
  6.5 0.8 add_bitcast_fusion
  7.3 1.2 %reshape.35 = bf16[16,64,64]{2,1,0:T(8,128)(2,1)S(1)} reshape(bf16[16,1,4096]{2,0,1:T(8,128)(2,1)} %param.6) | data formatting | bytes 262144 | tf_op jit(solution)/shard_map/reshape
  8.5 0.0 copy-done
  8.5 0.4 fusion.6
  8.9 1.8 %convolution_divide_fusion = f32[16,64,64]{2,1,0:T(8,128)S(1)} fusion(f32[16,64,64]{2,1,0:T(8,128)S(1)} %fusion.6, f32[64,64]{1,0:T(8,128)S(1)} %add_bitcast_fusion, f32[1,64,64]{2,1,0:T(8,128)} %param.7), kind=kOutput, calls=%fused_computation.2 | convolution fusion | flops 50397184 | bytes 557056 | tf_op jit(solution)/shard_map/lai,qlab,lbj->qlij/dot_general | solution.py:13
  10.7 0.6 fusion.4
  11.3 1.3 %convolution_convert_fusion = bf16[16,64,64]{2,1,0:T(8,128)(2,1)S(1)} fusion(f32[16,64,64]{1,2,0:T(8,128)S(1)} %fusion.4, f32[1,64,64]{2,1,0:T(8,128)} %param.7), kind=kOutput, calls=%fused_computation.3 | convolution fusion | flops 50397184 | bytes 409600 | tf_op jit(solution)/shard_map/lia,qlab,ljb->qlij/dot_general | solution.py:15
  12.7 0.9 %convert_element_type.8 = bf16[16,4096]{1,0:T(8,128)(2,1)} reshape(bf16[16,64,64]{2,1,0:T(8,128)(2,1)S(1)} %convolution_convert_fusion) | data formatting | bytes 262144 | tf_op jit(solution)/shard_map/convert_element_type | solution.py:16
  13.6 0.0 all-gather.2.cloned.1.call-update
  13.6 0.0 reduce-scatter.2.cloned.1.call-start
  13.7 44.0 %all-gather.2.cloned.1.call-done = bf16[256,4096]{1,0:T(8,128)(2,1)} async-done(((bf16[16,4096]{1,0:T(8,128)(2,1)}), bf16[256,4096]{1,0:T(8,128)(2,1)}) %all-gather.2.cloned.1.call-update) | async-done | bytes 2097168 | tf_op jit(solution)/shard_map/all_gather | solution.py:29
  57.7 4.9 %fusion = f32[256,512]{1,0:T(8,128)} fusion(bf16[256,4096]{1,0:T(8,128)(2,1)} %all-gather.2.cloned.1.call-done, bf16[512,1,4096]{2,0,1:T(8,128)(2,1)} %param.5), kind=kOutput, calls=%fused_computation | convolution fusion | flops 1073741824 | bytes 6815744 | tf_op jit(solution)/shard_map/dot_general | solution.py:20
  62.6 0.0 reduce-scatter.2.cloned.1.call-update
  62.6 13.1 %reduce-scatter.2.cloned.1.call-done = f32[128,512]{1,0:T(8,128)} async-done(((f32[256,512]{1,0:T(8,128)}), f32[128,512]{1,0:T(8,128)}) %reduce-scatter.2.cloned.1.call-update) | async-done | bytes 262160 | tf_op jit(solution)/shard_map/reduce_scatter | solution.py:30
  75.7 1.8 %copy.6 = f32[512,128]{1,0:T(8,128)} copy(f32[512,128]{0,1:T(8,128)} %bitcast.25) | data formatting | bytes 524288 | tf_op jit(solution)/shard_map/transpose | solution.py:33
Async XLA Ops:
  6.5 2.0 %copy-start = (f32[1,64,64]{2,1,0:T(8,128)S(1)}, f32[1,64,64]{2,1,0:T(8,128)}, u32[]{:S(2)}) copy-start(f32[1,64,64]{2,1,0:T(8,128)} %param.8) | copy-start | bytes 49156
  6.5 51.1 %all-gather.2.cloned.1.call-start = ((), (), s32[]{:S(2)}) async-start(), calls=%async_computation.1 | async-start | bytes 2228224 | tf_op jit(solution)/shard_map/all_gather | solution.py:29
  13.6 62.0 %reduce-scatter.2.cloned.1.call-start = ((), (), s32[]{:S(2)}) async-start(), calls=%async_computation.2 | async-start | bytes 786432 | tf_op jit(solution)/shard_map/reduce_scatter | solution.py:30
Sparse Core Ops, SparseCore 0:
  13.7 43.8 all-gather.1
  62.7 12.8 reduce-scatter.1
where the time goes:
time: 85.3 us; the launch traced here: 84.3 us
  waiting for transfers between devices  57.1 us (67%)
  between operations  13.4 us (16%)
  matrix products  9.02 us (11%)
  local copies, waits for them, and re-layouts  3.9 us (5%)
    all_gather x1, waiting for transfers between devices, body(): gathered = lax.all_gather(precond, 'shard', axis=0, tiled=True)  44 us
    reduce_scatter x1, waiting for transfers between devices, body(): lax.psum_scatter(score_block(gathered, train_flat), 'layer', scatter_dime...  13.1 us
    dot_general x1, matrix products, score_block(): lax.dot_general(left, right, (((1,), (1,)), ((), ())), preferred_element_...  4.9 us
    dot_general x2, matrix products, precondition(): jnp.einsum('lai,qlab,lbj->qlij', basis_out, grads, basis_in, precision=hi...  2.18 us
    dot_general x2, matrix products, precondition(): jnp.einsum('lia,qlab,ljb->qlij', basis_out, scaled, basis_in, precision=h...  1.93 us
    transpose x1, local copies, waits for them, and re-layouts, body(): return jnp.transpose(mine)  1.78 us
  transfers between devices with their start and end apart: 2, of which 2 were waited for; matrix products, arithmetic and copies ran while one was open for 0% of the time, Pallas kernels for 0%

commit v1 on v0

--- a/solution.py
+++ b/solution.py
@@ -1,7 +1,13 @@
+import functools
+
 import jax
 import jax.numpy as jnp
 from jax import lax
+from jax.experimental import pallas as pl
+from jax.experimental.pallas import tpu as pltpu
 from jax.sharding import PartitionSpec as P
+
+MESH = pl.DeviceIdType.MESH
 
 
 def precondition(queries, basis_in, basis_out, eigen):
@@ -22,10 +28,215 @@
     )
 
 
-def body(train_grads, queries, basis_in, basis_out, eigen):
+def kernel(depth, p_ref, t_hbm, o_ref, buf, train, own, outgoing, incoming,
+           load_sem, recv, send_right, send_left, send_y, send_core, recv_x, send_x):
+    me = lax.axis_index("shard")
+    layer = lax.axis_index("layer")
+    core = lax.rem(me, 2)
+    y = lax.rem(me // 2, 2)
+    z = me // 4
+    half = depth // 2
+    mine = y * 2 + core
+    across = (1 - y) * 2 + core
+    sibling = y * 2 + (1 - core)
+    diagonal = (1 - y) * 2 + (1 - core)
+
+    load = pltpu.make_async_copy(t_hbm, train, load_sem)
+    load.start()
+
+    barrier = pltpu.get_barrier_semaphore()
+    pl.semaphore_signal(barrier, inc=1, device_id={"shard": z * 4 + across}, device_id_type=MESH)
+    pl.semaphore_signal(barrier, inc=1, device_id={"shard": z * 4 + sibling}, device_id_type=MESH)
+    pl.semaphore_signal(barrier, inc=1, device_id={"layer": 1 - layer}, device_id_type=MESH)
+
+    @pl.when(z > 0)
+    def _():
+        pl.semaphore_signal(barrier, inc=1, device_id={"shard": me - 4}, device_id_type=MESH)
+
+    @pl.when(z < depth - 1)
+    def _():
+        pl.semaphore_signal(barrier, inc=1, device_id={"shard": me + 4}, device_id_type=MESH)
+
+    buf[z, mine] = p_ref[...]
+    pl.semaphore_wait(barrier, 3 + jnp.where(z > 0, 1, 0) + jnp.where(z < depth - 1, 1, 0))
+
+    def chunk(column, row, device, sem):
+        return pltpu.make_async_remote_copy(
+            src_ref=buf.at[column, row],
+            dst_ref=buf.at[column, row],
+            send_sem=sem,
+            recv_sem=recv.at[column, row],
+            device_id={"shard": device},
+            device_id_type=MESH,
+        )
+
+    def to_right(column):
+        return chunk(column, mine, me + 4, send_right.at[column])
+
+    def to_left(column):
+        return chunk(column, mine, me - 4, send_left.at[column])
+
+    def to_y(column):
+        return chunk(column, mine, z * 4 + across, send_y.at[column])
+
+    def to_core(column, row):
+        return chunk(column, row, z * 4 + sibling, send_core.at[column, row])
+
+    def arrived(column, row):
+        chunk(column, row, z * 4 + sibling, send_core.at[column, row]).wait_recv()
+
+    def partial_copy(slot):
+        return pltpu.make_async_remote_copy(
+            src_ref=outgoing.at[slot],
+            dst_ref=incoming.at[slot],
+            send_sem=send_x.at[slot],
+            recv_sem=recv_x.at[slot],
+            device_id={"layer": 1 - layer},
+            device_id_type=MESH,
+        )
+
+    def spread(column):
+        to_y(column).start()
+        to_core(column, mine).start()
+
+    def finish(column):
+        arrived(column, across)
+        to_core(column, across).start()
+        arrived(column, sibling)
+        arrived(column, diagonal)
+        block = score_block(buf[column].reshape(-1, buf.shape[-1]), train[...])
+        slot = lax.rem(column, half)
+        kept = column // half == layer
+
+        @pl.when(kept)
+        def _():
+            own[slot] = block
+
+        @pl.when(jnp.logical_not(kept))
+        def _():
+            outgoing[slot] = block.astype(outgoing.dtype)
+            partial_copy(slot).start()
+
+    @pl.when(z < depth - 1)
+    def _():
+        to_right(z).start()
+
+    @pl.when(z > 0)
+    def _():
+        to_left(z).start()
+
+    spread(z)
+
+    for step in range(1, depth):
+        @pl.when(z >= step)
+        def _():
+            column = z - step
+            arrived(column, mine)
+
+            @pl.when(z < depth - 1)
+            def _():
+                to_right(column).start()
+
+            spread(column)
+
+        @pl.when(z + step < depth)
+        def _():
+            column = z + step
+            arrived(column, mine)
+
+            @pl.when(z > 0)
+            def _():
+                to_left(column).start()
+
+            spread(column)
+
+        if step == 1:
+            load.wait()
+            finish(z)
+        else:
+            back = step - 1
+
+            @pl.when(z >= back)
+            def _():
+                finish(z - back)
+
+            @pl.when(z + back < depth)
+            def _():
+                finish(z + back)
+
+    back = depth - 1
+
+    @pl.when(z >= back)
+    def _():
+        finish(z - back)
+
+    @pl.when(z + back < depth)
+    def _():
+        finish(z + back)
+
+    for slot in range(half):
+        partial_copy(slot).wait_recv()
+        total = own[slot] + incoming[slot].astype(jnp.float32)
+        own[slot] = total
+    o_ref[...] = own[...].reshape(-1, own.shape[-1]).T
+
+    for slot in range(half):
+        partial_copy(slot).wait_send()
+    for column in range(depth):
+        to_y(column).wait_send()
+        to_core(column, mine).wait_send()
+        to_core(column, across).wait_send()
+
+        @pl.when(jnp.logical_and(z >= column, z < depth - 1))
+        def _():
+            to_right(column).wait_send()
+
+        @pl.when(jnp.logical_and(z <= column, z > 0))
+        def _():
+            to_left(column).wait_send()
+
+
+def fused_scores(precond, train_flat, shards):
+    count, width = precond.shape
+    examples = train_flat.shape[0]
+    depth = shards // 4
+    half = depth // 2
+    dma = pltpu.SemaphoreType.DMA
+    return pl.pallas_call(
+        functools.partial(kernel, depth),
+        out_shape=jax.ShapeDtypeStruct((examples, half * 4 * count), jnp.float32),
+        in_specs=[
+            pl.BlockSpec(memory_space=pltpu.VMEM),
+            pl.BlockSpec(memory_space=pl.ANY),
+        ],
+        out_specs=pl.BlockSpec(memory_space=pltpu.VMEM),
+        scratch_shapes=[
+            pltpu.VMEM((depth, 4, count, width), jnp.bfloat16),
+            pltpu.VMEM((examples, width), jnp.bfloat16),
+            pltpu.VMEM((half, 4 * count, examples), jnp.float32),
+            pltpu.VMEM((half, 4 * count, examples), jnp.bfloat16),
+            pltpu.VMEM((half, 4 * count, examples), jnp.bfloat16),
+            dma,
+            dma((depth, 4)),
+            dma((depth,)),
+            dma((depth,)),
+            dma((depth,)),
+            dma((depth, 4)),
+            dma((half,)),
+            dma((half,)),
+        ],
+        compiler_params=pltpu.CompilerParams(
+            collective_id=0, has_side_effects=True, vmem_limit_bytes=48 * 1024 * 1024
+        ),
+    )(precond, train_flat)
+
+
+def body(fused, shards, train_grads, queries, basis_in, basis_out, eigen):
     examples = train_grads.shape[0]
     train_flat = train_grads.reshape(examples, train_grads.shape[1] * train_grads.shape[2])
     precond = precondition(queries, basis_in, basis_out, eigen)
+    if fused:
+        return fused_scores(precond, train_flat, shards)
     gathered = lax.all_gather(precond, "shard", axis=0, tiled=True)
     mine = lax.psum_scatter(
         score_block(gathered, train_flat), "layer", scatter_dimension=0, tiled=True
@@ -41,6 +252,9 @@
         P("layer", None, None),
         P("layer", None, None),
     )
+    shards = mesh.shape["shard"]
+    fused = mesh.shape["groups"] == 1 and mesh.shape["layer"] == 2 and shards == 16
     return jax.shard_map(
-        body, mesh=mesh, in_specs=placed, out_specs=P(("groups", "shard"), "layer"), check_vma=False
-    )
+        functools.partial(body, fused, shards), mesh=mesh, in_specs=placed,
+        out_specs=P(("groups", "shard"), "layer"), check_vma=False
+    )

time: 85.3 us -> 35.3 us (0.41)
  waiting for transfers between devices: 57.1 us -> 0 us
  Pallas kernels: 0 us -> 25.6 us
  between operations: 13.4 us -> 0.06 us
  matrix products: 9.02 us -> 4.12 us
    all_gather x1 -> x0, waiting for transfers between devices: 44 us -> none  [body(): gathered = lax.all_gather(precond, 'shard', axis=0, tiled=True)]
    pallas_call x0 -> x1, Pallas kernels: none -> 25.6 us  [fused_scores(): pl.pallas_call(functools.partial(kernel, depth), out_shape=jax.ShapeDtype...]
    reduce_scatter x1 -> x0, waiting for transfers between devices: 13.1 us -> none  [body(): lax.psum_scatter(score_block(gathered, train_flat), 'layer', scatter_dime...]
    dot_general x1 -> x0, matrix products: 4.9 us -> none  [score_block(): lax.dot_general(left, right, (((1,), (1,)), ((), ())), preferred_element_...]
    unnamed x2 -> x5, local copies, waits for them, and re-layouts: 0.01 us -> 2.9 us
    transpose x1 -> x0, local copies, waits for them, and re-layouts: 1.78 us -> none  [body(): return jnp.transpose(mine)]
  transfers between devices with their start and end apart: 2 -> 0, of which waited for: 2 -> 0; matrix products, arithmetic and copies ran while one was open for 0% -> 0% of each run, Pallas kernels for 0% -> 0%
where the time goes in v1:
time: 35.3 us; the launch traced here: 34.9 us
  Pallas kernels  25.6 us (73%)
  local copies, waits for them, and re-layouts  4.35 us (12%)
  matrix products  4.12 us (12%)
  other arithmetic  0.77 us (2%)
    pallas_call x1, Pallas kernels, fused_scores(): pl.pallas_call(functools.partial(kernel, depth), out_shape=jax.ShapeDtype...  25.6 us
    unnamed x5, local copies, waits for them, and re-layouts  2.9 us
    dot_general x2, matrix products, precondition(): jnp.einsum('lai,qlab,lbj->qlij', basis_out, grads, basis_in, precision=hi...  2.18 us
    dot_general x2, matrix products, precondition(): jnp.einsum('lia,qlab,ljb->qlij', basis_out, scaled, basis_in, precision=h...  1.94 us
    reshape x1, local copies, waits for them, and re-layouts  1.18 us
    div x1, other arithmetic, precondition(): scaled = rotated / (eigen + 0.1)  0.77 us

profile of v1, /device:TPU:1, one launch (start us, length us, event | category | flops | bytes accessed | tf_op | source)
XLA Modules:
  0.0 34.9 jit_solution(3030055983164967614)
XLA Ops:
  0.0 0.0 copy-start
  0.0 0.8 %add_bitcast_fusion = f32[64,64]{1,0:T(8,128)S(1)} fusion(f32[1,64,64]{2,1,0:T(8,128)} %param.9), kind=kLoop, calls=%fused_computation.8 | loop fusion | flops 4096 | bytes 32768 | tf_op jit(solution)/shard_map/div | solution.py:20
  0.8 1.2 %reshape.35 = bf16[16,64,64]{2,1,0:T(8,128)(2,1)S(1)} reshape(bf16[16,1,4096]{2,0,1:T(8,128)(2,1)} %param.6) | data formatting | bytes 262144 | tf_op jit(solution)/shard_map/reshape
  2.0 0.0 copy-done
  2.0 0.4 %fusion.4 = f32[16,64,64]{2,1,0:T(8,128)S(1)} fusion(bf16[16,64,64]{2,1,0:T(8,128)(2,1)S(1)} %reshape.35, f32[1,64,64]{2,1,0:T(8,128)S(1)} %copy-done), kind=kOutput, calls=%fused_computation.6 | convolution fusion | flops 50331648 | bytes 409600 | tf_op jit(solution)/shard_map/lai,qlab,lbj->qlij/dot_general | solution.py:19
  2.4 1.8 %convolution_divide_fusion = f32[16,64,64]{2,1,0:T(8,128)S(1)} fusion(f32[16,64,64]{2,1,0:T(8,128)S(1)} %fusion.4, f32[64,64]{1,0:T(8,128)S(1)} %add_bitcast_fusion, f32[1,64,64]{2,1,0:T(8,128)} %param.7), kind=kOutput, calls=%fused_computation | convolution fusion | flops 50397184 | bytes 557056 | tf_op jit(solution)/shard_map/lai,qlab,lbj->qlij/dot_general | solution.py:19
  4.2 0.6 %fusion.2 = f32[16,64,64]{1,2,0:T(8,128)S(1)} fusion(f32[16,64,64]{2,1,0:T(8,128)S(1)} %convolution_divide_fusion, f32[1,64,64]{2,1,0:T(8,128)S(1)} %copy-done), kind=kOutput, calls=%fused_computation.4 | convolution fusion | flops 50331648 | bytes 540672 | tf_op jit(solution)/shard_map/lia,qlab,ljb->qlij/dot_general | solution.py:21
  4.8 1.3 %convolution_convert_fusion = bf16[16,64,64]{2,1,0:T(8,128)(2,1)S(1)} fusion(f32[16,64,64]{1,2,0:T(8,128)S(1)} %fusion.2, f32[1,64,64]{2,1,0:T(8,128)} %param.7), kind=kOutput, calls=%fused_computation.1 | convolution fusion | flops 50397184 | bytes 409600 | tf_op jit(solution)/shard_map/lia,qlab,ljb->qlij/dot_general | solution.py:21
  6.1 0.3 convert_element_type.7.p_ref
  6.4 0.0 copy-start.1
  6.4 2.2 %copy-done.1 = bf16[512,1,4096]{2,0,1:T(8,128)(2,1)S(1)} copy-done((bf16[512,1,4096]{2,0,1:T(8,128)(2,1)S(1)}, bf16[512,1,4096]{2,0,1:T(8,128)(2,1)}, u32[]{:S(2)}) %copy-start.1) | copy-done | bytes 4194328
  8.6 25.6 %shard_map.55 = f32[512,128]{1,0:T(8,128)S(1)} custom-call(bf16[16,4096]{1,0:T(8,128)(2,1)S(1)} %convert_element_type.7.p_ref, bf16[512,4096]{1,0:T(8,128)(2,1)S(1)} %bitcast.21), custom_call_target="tpu_custom_call" | custom-call | tf_op jit(solution)/shard_map/pallas_call | solution.py:205
  34.2 0.7 %copy.7 = f32[512,128]{1,0:T(8,128)} copy(f32[512,128]{1,0:T(8,128)S(1)} %shard_map.55) | data formatting | bytes 524288
Async XLA Ops:
  0.0 2.0 %copy-start = (f32[1,64,64]{2,1,0:T(8,128)S(1)}, f32[1,64,64]{2,1,0:T(8,128)}, u32[]{:S(2)}) copy-start(f32[1,64,64]{2,1,0:T(8,128)} %param.8) | copy-start | bytes 49156
  6.4 2.2 %copy-start.1 = (bf16[512,1,4096]{2,0,1:T(8,128)(2,1)S(1)}, bf16[512,1,4096]{2,0,1:T(8,128)(2,1)}, u32[]{:S(2)}) copy-start(bf16[512,1,4096]{2,0,1:T(8,128)(2,1)} %param.5) | copy-start | bytes 12582916

commit v2 on v1

--- a/solution.py
+++ b/solution.py
@@ -28,7 +28,90 @@
     )
 
 
-def kernel(depth, p_ref, t_hbm, o_ref, buf, train, own, outgoing, incoming,
+def split(value):
+    high = value.astype(jnp.bfloat16)
+    return high, (value - high.astype(jnp.float32)).astype(jnp.bfloat16)
+
+
+def dot(left, right):
+    return jnp.dot(left, right, preferred_element_type=jnp.float32)
+
+
+def twice_diagonal(block):
+    empty = jnp.zeros_like(block)
+    return jnp.concatenate(
+        [jnp.concatenate([block, empty], 1), jnp.concatenate([empty, block], 1)], 0
+    )
+
+
+def swap_halves(value, side):
+    return pltpu.roll(value, side, 1)
+
+
+def precondition_block(q_ref, basis_in_ref, basis_out_ref, eigen_ref, rows_ref, store):
+    count = q_ref.shape[0]
+    side = basis_in_ref.shape[-1]
+    lanes = 2 * side
+    tiles = side // 2
+    lower = lax.broadcasted_iota(jnp.int32, (tiles, lanes), 1) < side
+
+    basis_in = basis_in_ref[...]
+    in_high, in_low = split(twice_diagonal(basis_in))
+    back_high, back_low = split(twice_diagonal(basis_in.T))
+    ordered = jnp.concatenate(
+        [basis_out_ref[pl.ds(0, tiles, stride=2), :], basis_out_ref[pl.ds(1, tiles, stride=2), :]], 0
+    )
+    out_high, out_low = split(ordered)
+    turn_high, turn_low = split(ordered.T)
+    inverse = 1.0 / (eigen_ref[...] + 0.1)
+    inverse = jnp.concatenate([inverse, inverse], 1)
+
+    stacked = jnp.concatenate(
+        [q_ref[:, t * lanes:(t + 1) * lanes] for t in range(tiles)], 0
+    )
+    both = dot(stacked, jnp.concatenate([in_high, in_low], 1))
+    rows_ref[...] = both[:, :lanes] + both[:, lanes:]
+
+    pairs = []
+    for pair in range(count // 2):
+        first = rows_ref[pl.ds(2 * pair, tiles, stride=count), :]
+        second = rows_ref[pl.ds(2 * pair + 1, tiles, stride=count), :]
+        even = jnp.where(lower, first, swap_halves(second, side))
+        odd = jnp.where(lower, swap_halves(first, side), second)
+        pairs.append(jnp.concatenate([even, odd], 0))
+    high, low = split(jnp.concatenate(pairs, 1))
+    rotated = dot(
+        jnp.concatenate([turn_high, turn_high, turn_low], 1), jnp.concatenate([high, low, high], 0)
+    )
+    scaled = rotated * jnp.concatenate([inverse] * (count // 2), 1)
+    high, low = split(scaled)
+    lifted = dot(
+        jnp.concatenate([out_high, out_high, out_low], 1), jnp.concatenate([high, low, high], 0)
+    )
+    queries = []
+    for pair in range(count // 2):
+        even = lifted[:tiles, pair * lanes:(pair + 1) * lanes]
+        odd = lifted[tiles:, pair * lanes:(pair + 1) * lanes]
+        queries.append(jnp.where(lower, even, swap_halves(odd, side)))
+        queries.append(jnp.where(lower, swap_halves(even, side), odd))
+    high, low = split(jnp.concatenate(queries, 0))
+    both = dot(
+        jnp.concatenate([high, low], 1),
+        jnp.concatenate(
+            [
+                jnp.concatenate([back_high, back_low], 1),
+                jnp.concatenate([back_high, jnp.zeros_like(back_low)], 1),
+            ],
+            0,
+        ),
+    )
+    rows_ref[...] = both[:, :lanes] + both[:, lanes:]
+    for t in range(tiles):
+        store(t, rows_ref[pl.ds(t, count, stride=tiles), :].astype(jnp.bfloat16))
+
+
+def kernel(depth, q_hbm, basis_in_hbm, basis_out_hbm, eigen_hbm, t_hbm, o_ref,
+           queries, basis_in, basis_out, eigen, rows, buf, train, own, outgoing, incoming,
            load_sem, recv, send_right, send_left, send_y, send_core, recv_x, send_x):
     me = lax.axis_index("shard")
     layer = lax.axis_index("layer")
@@ -41,7 +124,15 @@
     sibling = y * 2 + (1 - core)
     diagonal = (1 - y) * 2 + (1 - core)
 
-    load = pltpu.make_async_copy(t_hbm, train, load_sem)
+    smalls = [
+        pltpu.make_async_copy(source, target, load_sem.at[index])
+        for index, (source, target) in enumerate(
+            [(q_hbm, queries), (basis_in_hbm, basis_in), (basis_out_hbm, basis_out), (eigen_hbm, eigen)]
+        )
+    ]
+    for small in smalls:
+        small.start()
+    load = pltpu.make_async_copy(t_hbm, train, load_sem.at[len(smalls)])
     load.start()
 
     barrier = pltpu.get_barrier_semaphore()
@@ -57,7 +148,13 @@
     def _():
         pl.semaphore_signal(barrier, inc=1, device_id={"shard": me + 4}, device_id_type=MESH)
 
-    buf[z, mine] = p_ref[...]
+    for small in smalls:
+        small.wait()
+
+    def store(tile, value):
+        buf[z, mine, :, tile * value.shape[1]:(tile + 1) * value.shape[1]] = value
+
+    precondition_block(queries, basis_in, basis_out, eigen, rows, store)
     pl.semaphore_wait(barrier, 3 + jnp.where(z > 0, 1, 0) + jnp.where(z < depth - 1, 1, 0))
 
     def chunk(column, row, device, sem):
@@ -196,8 +293,9 @@
             to_left(column).wait_send()
 
 
-def fused_scores(precond, train_flat, shards):
-    count, width = precond.shape
+def fused_scores(queries, basis_in, basis_out, eigen, train_flat, shards):
+    count, width = queries.shape
+    side = basis_in.shape[-1]
     examples = train_flat.shape[0]
     depth = shards // 4
     half = depth // 2
@@ -205,18 +303,20 @@
     return pl.pallas_call(
         functools.partial(kernel, depth),
         out_shape=jax.ShapeDtypeStruct((examples, half * 4 * count), jnp.float32),
-        in_specs=[
-            pl.BlockSpec(memory_space=pltpu.VMEM),
-            pl.BlockSpec(memory_space=pl.ANY),
-        ],
+        in_specs=[pl.BlockSpec(memory_space=pl.ANY)] * 5,
         out_specs=pl.BlockSpec(memory_space=pltpu.VMEM),
         scratch_shapes=[
+            pltpu.VMEM((count, width), jnp.bfloat16),
+            pltpu.VMEM((side, side), jnp.float32),
+            pltpu.VMEM((side, side), jnp.float32),
+            pltpu.VMEM((side, side), jnp.float32),
+            pltpu.VMEM((count * side // 2, 2 * side), jnp.float32),
             pltpu.VMEM((depth, 4, count, width), jnp.bfloat16),
             pltpu.VMEM((examples, width), jnp.bfloat16),
             pltpu.VMEM((half, 4 * count, examples), jnp.float32),
             pltpu.VMEM((half, 4 * count, examples), jnp.bfloat16),
             pltpu.VMEM((half, 4 * count, examples), jnp.bfloat16),
-            dma,
+            dma((5,)),
             dma((depth, 4)),
             dma((depth,)),
             dma((depth,)),
@@ -226,17 +326,19 @@
             dma((half,)),
         ],
         compiler_params=pltpu.CompilerParams(
-            collective_id=0, has_side_effects=True, vmem_limit_bytes=48 * 1024 * 1024
+            collective_id=0, has_side_effects=True, vmem_limit_bytes=60 * 1024 * 1024
         ),
-    )(precond, train_flat)
+    )(queries, basis_in, basis_out, eigen, train_flat)
 
 
 def body(fused, shards, train_grads, queries, basis_in, basis_out, eigen):
     examples = train_grads.shape[0]
     train_flat = train_grads.reshape(examples, train_grads.shape[1] * train_grads.shape[2])
+    if fused:
+        return fused_scores(
+            queries.reshape(queries.shape[0], -1), basis_in[0], basis_out[0], eigen[0], train_flat, shards
+        )
     precond = precondition(queries, basis_in, basis_out, eigen)
-    if fused:
-        return fused_scores(precond, train_flat, shards)
     gathered = lax.all_gather(precond, "shard", axis=0, tiled=True)
     mine = lax.psum_scatter(
         score_block(gathered, train_flat), "layer", scatter_dimension=0, tiled=True

time: 35.3 us -> 29 us (0.82)
  matrix products: 4.12 us -> 0 us
  local copies, waits for them, and re-layouts: 4.35 us -> 1.67 us
  Pallas kernels: 25.6 us -> 27 us
  other arithmetic: 0.77 us -> 0 us
    dot_general x4 -> x0, matrix products: 4.12 us -> none  [the longest x2 2.18 us: precondition(): jnp.einsum('lai,qlab,lbj->qlij', basis_out, grads, basis_in, precision=hi...]
    pallas_call x1, Pallas kernels: 25.6 us -> 27 us  [fused_scores(): pl.pallas_call(functools.partial(kernel, depth), out_shape=jax.ShapeDtype...]
    unnamed x5 -> x1, local copies, waits for them, and re-layouts: 2.9 us -> 1.67 us
    reshape x1 -> x0, local copies, waits for them, and re-layouts: 1.18 us -> none
    div x1 -> x0, other arithmetic: 0.77 us -> none  [precondition(): scaled = rotated / (eigen + 0.1)]
where the time goes in v2:
time: 29 us; the launch traced here: 28.7 us
  Pallas kernels  27 us (93%)
  local copies, waits for them, and re-layouts  1.67 us (6%)
    pallas_call x1, Pallas kernels, fused_scores(): pl.pallas_call(functools.partial(kernel, depth), out_shape=jax.ShapeDtype...  27 us
    unnamed x1, local copies, waits for them, and re-layouts  1.67 us

profile of v2, /device:TPU:1, one launch (start us, length us, event | category | flops | bytes accessed | tf_op | source)
XLA Modules:
  0.0 28.7 jit_solution(6728210110074868363)
XLA Ops:
  0.0 27.0 %shard_map.55 = f32[512,128]{1,0:T(8,128)} custom-call(bf16[16,4096]{1,0:T(8,128)(2,1)} %bitcast.6, f32[64,64]{1,0:T(8,128)} %bitcast.7, f32[64,64]{1,0:T(8,128)} %bitcast.8, f32[64,64]{1,0:T(8,128)} %bitcast.9, bf16[512,4096]{1,0:T(8,128)(2,1)} %bitcast.5), custom_call_target="tpu_custom_call" | custom-call | tf_op jit(solution)/shard_map/pallas_call | solution.py:303
  27.0 1.7 %copy.7 = f32[512,128]{1,0:T(8,128)} copy(f32[512,128]{1,0:T(8,128)} %shard_map.55) | data formatting | bytes 524288

commit v3 on v2

--- a/solution.py
+++ b/solution.py
@@ -8,6 +8,7 @@
 from jax.sharding import PartitionSpec as P
 
 MESH = pl.DeviceIdType.MESH
+PIECES = 2
 
 
 def precondition(queries, basis_in, basis_out, eigen):
@@ -110,9 +111,9 @@
         store(t, rows_ref[pl.ds(t, count, stride=tiles), :].astype(jnp.bfloat16))
 
 
-def kernel(depth, q_hbm, basis_in_hbm, basis_out_hbm, eigen_hbm, t_hbm, o_ref,
+def kernel(depth, pieces, q_hbm, basis_in_hbm, basis_out_hbm, eigen_hbm, t_hbm, o_ref,
            queries, basis_in, basis_out, eigen, rows, buf, train, own, outgoing, incoming,
-           load_sem, recv, send_right, send_left, send_y, send_core, recv_x, send_x):
+           load_sem, recv, recv_core, send_right, send_left, send_y, send_core, recv_x, send_x):
     me = lax.axis_index("shard")
     layer = lax.axis_index("layer")
     core = lax.rem(me, 2)
@@ -152,35 +153,47 @@
         small.wait()
 
     def store(tile, value):
-        buf[z, mine, :, tile * value.shape[1]:(tile + 1) * value.shape[1]] = value
+        per = buf.shape[-1] // value.shape[1]
+        at = tile % per * value.shape[1]
+        buf[z, mine, tile // per, :, at:at + value.shape[1]] = value
 
     precondition_block(queries, basis_in, basis_out, eigen, rows, store)
     pl.semaphore_wait(barrier, 3 + jnp.where(z > 0, 1, 0) + jnp.where(z < depth - 1, 1, 0))
 
-    def chunk(column, row, device, sem):
+    def chunk(column, row, piece, device, sem):
+        return pltpu.make_async_remote_copy(
+            src_ref=buf.at[column, row, piece],
+            dst_ref=buf.at[column, row, piece],
+            send_sem=sem,
+            recv_sem=recv.at[column, row, piece],
+            device_id={"shard": device},
+            device_id_type=MESH,
+        )
+
+    def to_right(column, piece):
+        return chunk(column, mine, piece, me + 4, send_right.at[column])
+
+    def to_left(column, piece):
+        return chunk(column, mine, piece, me - 4, send_left.at[column])
+
+    def to_y(column, piece):
+        return chunk(column, mine, piece, z * 4 + across, send_y.at[0])
+
+    def to_core(column, row):
         return pltpu.make_async_remote_copy(
             src_ref=buf.at[column, row],
             dst_ref=buf.at[column, row],
-            send_sem=sem,
-            recv_sem=recv.at[column, row],
-            device_id={"shard": device},
+            send_sem=send_core.at[0],
+            recv_sem=recv_core.at[column, row],
+            device_id={"shard": z * 4 + sibling},
             device_id_type=MESH,
         )
 
-    def to_right(column):
-        return chunk(column, mine, me + 4, send_right.at[column])
-
-    def to_left(column):
-        return chunk(column, mine, me - 4, send_left.at[column])
-
-    def to_y(column):
-        return chunk(column, mine, z * 4 + across, send_y.at[column])
-
-    def to_core(column, row):
-        return chunk(column, row, z * 4 + sibling, send_core.at[column, row])
-
-    def arrived(column, row):
-        chunk(column, row, z * 4 + sibling, send_core.at[column, row]).wait_recv()
+    def arrived(column, row, piece):
+        chunk(column, row, piece, z * 4 + across, send_y.at[0]).wait_recv()
+
+    def sent(region, sem):
+        pltpu.make_async_copy(region, region, sem).wait()
 
     def partial_copy(slot):
         return pltpu.make_async_remote_copy(
@@ -192,16 +205,39 @@
             device_id_type=MESH,
         )
 
-    def spread(column):
-        to_y(column).start()
-        to_core(column, mine).start()
-
-    def finish(column):
-        arrived(column, across)
-        to_core(column, across).start()
-        arrived(column, sibling)
-        arrived(column, diagonal)
-        block = score_block(buf[column].reshape(-1, buf.shape[-1]), train[...])
+    def along(column, piece):
+        @pl.when(jnp.logical_and(column <= z, z < depth - 1))
+        def _():
+            to_right(column, piece).start()
+
+        @pl.when(jnp.logical_and(column >= z, z > 0))
+        def _():
+            to_left(column, piece).start()
+
+        to_y(column, piece).start()
+        if piece == pieces - 1:
+            to_core(column, mine).start()
+
+    def from_row(column, piece):
+        arrived(column, mine, piece)
+        along(column, piece)
+
+    def from_across(column, piece):
+        arrived(column, across, piece)
+        if piece == pieces - 1:
+            to_core(column, across).start()
+
+    def multiply(column):
+        block = None
+        to_core(column, sibling).wait_recv()
+        to_core(column, diagonal).wait_recv()
+        for piece in range(pieces):
+            depth_of = buf.shape[-1]
+            term = score_block(
+                buf[column, :, piece].reshape(-1, depth_of),
+                train[:, piece * depth_of:(piece + 1) * depth_of],
+            )
+            block = term if block is None else block + term
         slot = lax.rem(column, half)
         kept = column // half == layer
 
@@ -214,62 +250,44 @@
             outgoing[slot] = block.astype(outgoing.dtype)
             partial_copy(slot).start()
 
-    @pl.when(z < depth - 1)
-    def _():
-        to_right(z).start()
-
-    @pl.when(z > 0)
-    def _():
-        to_left(z).start()
-
-    spread(z)
-
+    def at_distance(step, act):
+        if step == 0:
+            act(z)
+            return
+
+        @pl.when(z >= step)
+        def _():
+            act(z - step)
+
+        @pl.when(z + step < depth)
+        def _():
+            act(z + step)
+
+    for piece in range(pieces):
+        along(z, piece)
     for step in range(1, depth):
-        @pl.when(z >= step)
-        def _():
-            column = z - step
-            arrived(column, mine)
-
-            @pl.when(z < depth - 1)
-            def _():
-                to_right(column).start()
-
-            spread(column)
-
-        @pl.when(z + step < depth)
-        def _():
-            column = z + step
-            arrived(column, mine)
-
-            @pl.when(z > 0)
-            def _():
-                to_left(column).start()
-
-            spread(column)
-
-        if step == 1:
+        for piece in range(pieces):
+            at_distance(step, functools.partial(from_row, piece=piece))
+            at_distance(step - 1, functools.partial(from_across, piece=piece))
+        if step == 2:
             load.wait()
-            finish(z)
-        else:
-            back = step - 1
-
-            @pl.when(z >= back)
-            def _():
-                finish(z - back)
-
-            @pl.when(z + back < depth)
-            def _():
-                finish(z + back)
-
-    back = depth - 1
-
-    @pl.when(z >= back)
-    def _():
-        finish(z - back)
-
-    @pl.when(z + back < depth)
-    def _():
-        finish(z + back)
+        if step >= 2:
+            at_distance(step - 2, multiply)
+    at_distance(depth - 2, multiply)
+    for piece in range(pieces):
+        at_distance(depth - 1, functools.partial(from_across, piece=piece))
+    at_distance(depth - 1, multiply)
+
+    sent(buf.at[:, mine], send_y.at[0])
+    sent(buf.at[:, pl.ds(0, 2)], send_core.at[0])
+    for column in range(depth):
+        @pl.when(jnp.logical_and(z >= column, z < depth - 1))
+        def _():
+            sent(buf.at[column, mine], send_right.at[column])
+
+        @pl.when(jnp.logical_and(z <= column, z > 0))
+        def _():
+            sent(buf.at[column, mine], send_left.at[column])
 
     for slot in range(half):
         partial_copy(slot).wait_recv()
@@ -279,18 +297,6 @@
 
     for slot in range(half):
         partial_copy(slot).wait_send()
-    for column in range(depth):
-        to_y(column).wait_send()
-        to_core(column, mine).wait_send()
-        to_core(column, across).wait_send()
-
-        @pl.when(jnp.logical_and(z >= column, z < depth - 1))
-        def _():
-            to_right(column).wait_send()
-
-        @pl.when(jnp.logical_and(z <= column, z > 0))
-        def _():
-            to_left(column).wait_send()
 
 
 def fused_scores(queries, basis_in, basis_out, eigen, train_flat, shards):
@@ -299,9 +305,10 @@
     examples = train_flat.shape[0]
     depth = shards // 4
     half = depth // 2
+    pieces = PIECES
     dma = pltpu.SemaphoreType.DMA
     return pl.pallas_call(
-        functools.partial(kernel, depth),
+        functools.partial(kernel, depth, pieces),
         out_shape=jax.ShapeDtypeStruct((examples, half * 4 * count), jnp.float32),
         in_specs=[pl.BlockSpec(memory_space=pl.ANY)] * 5,
         out_specs=pl.BlockSpec(memory_space=pltpu.VMEM),
@@ -311,17 +318,18 @@
             pltpu.VMEM((side, side), jnp.float32),
             pltpu.VMEM((side, side), jnp.float32),
             pltpu.VMEM((count * side // 2, 2 * side), jnp.float32),
-            pltpu.VMEM((depth, 4, count, width), jnp.bfloat16),
+            pltpu.VMEM((depth, 4, pieces, count, width // pieces), jnp.bfloat16),
             pltpu.VMEM((examples, width), jnp.bfloat16),
             pltpu.VMEM((half, 4 * count, examples), jnp.float32),
             pltpu.VMEM((half, 4 * count, examples), jnp.bfloat16),
             pltpu.VMEM((half, 4 * count, examples), jnp.bfloat16),
             dma((5,)),
+            dma((depth, 4, pieces)),
             dma((depth, 4)),
             dma((depth,)),
             dma((depth,)),
-            dma((depth,)),
-            dma((depth, 4)),
+            dma((1,)),
+            dma((1,)),
             dma((half,)),
             dma((half,)),
         ],

time: 29 us -> 27.5 us (0.948)
  Pallas kernels: 27 us -> 25.6 us
    pallas_call x1, Pallas kernels: 27 us -> 25.6 us  [fused_scores(): pl.pallas_call(functools.partial(kernel, depth, pieces), out_shape=jax.Sh...]
where the time goes in v3:
time: 27.5 us; the launch traced here: 27.3 us
  Pallas kernels  25.6 us (93%)
  local copies, waits for them, and re-layouts  1.67 us (6%)
    pallas_call x1, Pallas kernels, fused_scores(): pl.pallas_call(functools.partial(kernel, depth, pieces), out_shape=jax.Sh...  25.6 us
    unnamed x1, local copies, waits for them, and re-layouts  1.67 us

profile of v3, /device:TPU:1, one launch (start us, length us, event | category | flops | bytes accessed | tf_op | source)
XLA Modules:
  0.0 27.3 jit_solution(15950407124815166268)
XLA Ops:
  0.0 25.6 %shard_map.55 = f32[512,128]{1,0:T(8,128)} custom-call(bf16[16,4096]{1,0:T(8,128)(2,1)} %bitcast.6, f32[64,64]{1,0:T(8,128)} %bitcast.7, f32[64,64]{1,0:T(8,128)} %bitcast.8, f32[64,64]{1,0:T(8,128)} %bitcast.9, bf16[512,4096]{1,0:T(8,128)(2,1)} %bitcast.5), custom_call_target="tpu_custom_call" | custom-call | tf_op jit(solution)/shard_map/pallas_call | solution.py:310
  25.6 1.7 %copy.7 = f32[512,128]{1,0:T(8,128)} copy(f32[512,128]{1,0:T(8,128)} %shard_map.55) | data formatting | bytes 524288

commit v4 on v3

--- a/solution.py
+++ b/solution.py
@@ -234,10 +234,11 @@
         for piece in range(pieces):
             depth_of = buf.shape[-1]
             term = score_block(
+                train[:, piece * depth_of:(piece + 1) * depth_of],
                 buf[column, :, piece].reshape(-1, depth_of),
-                train[:, piece * depth_of:(piece + 1) * depth_of],
             )
             block = term if block is None else block + term
+        block = block.T
         slot = lax.rem(column, half)
         kept = column // half == layer
 

time: 27.5 us -> 27.1 us (0.985)
  Pallas kernels: 25.6 us -> 25.2 us
    pallas_call x1, Pallas kernels: 25.6 us -> 25.2 us  [fused_scores(): pl.pallas_call(functools.partial(kernel, depth, pieces), out_shape=jax.Sh...]
where the time goes in v4:
time: 27.1 us; the launch traced here: 26.8 us
  Pallas kernels  25.2 us (93%)
  local copies, waits for them, and re-layouts  1.67 us (6%)
    pallas_call x1, Pallas kernels, fused_scores(): pl.pallas_call(functools.partial(kernel, depth, pieces), out_shape=jax.Sh...  25.2 us
    unnamed x1, local copies, waits for them, and re-layouts  1.67 us

profile of v4, /device:TPU:1, one launch (start us, length us, event | category | flops | bytes accessed | tf_op | source)
XLA Modules:
  0.0 26.8 jit_solution(239681765457596131)
XLA Ops:
  0.0 25.2 %shard_map.55 = f32[512,128]{1,0:T(8,128)} custom-call(bf16[16,4096]{1,0:T(8,128)(2,1)} %bitcast.6, f32[64,64]{1,0:T(8,128)} %bitcast.7, f32[64,64]{1,0:T(8,128)} %bitcast.8, f32[64,64]{1,0:T(8,128)} %bitcast.9, bf16[512,4096]{1,0:T(8,128)(2,1)} %bitcast.5), custom_call_target="tpu_custom_call" | custom-call | tf_op jit(solution)/shard_map/pallas_call | solution.py:311
  25.2 1.7 %copy.7 = f32[512,128]{1,0:T(8,128)} copy(f32[512,128]{1,0:T(8,128)} %shard_map.55) | data formatting | bytes 524288
